TPU v7x, 256 devices: a whole 4x4x8 slice. The times are simulated.
256 devices in a mesh: row: 32 (over z_hi, x, core), col: 8 (over y, z_lo).
Axes of the slice: x: 4, y: 4, z: 8 (z_hi: 4, z_lo: 2; z = z_hi * 2 + z_lo), core: 2. Of those that a mesh axis runs over, the one named last changes fastest.
Arguments:
- row_features: bfloat16 [512, 256], P(('row', 'col')), may hold values from -6 to 6
- col_features: bfloat16 [2048, 256], P(('col', 'row')), may hold values from -6 to 6
- row_proj: bfloat16 [256, 64], replicated, may hold values from -0.375 to 0.375
- col_proj: bfloat16 [256, 64], replicated, may hold values from -0.375 to 0.375
- pair_weight: bfloat16 [2, 3, 3, 64, 64], replicated, may hold values from -0.1875 to 0.1875
- pair_bias: float32 [64], replicated, may hold values from -4 to 4
- conv_weight: bfloat16 [3, 3, 64, 64], replicated, may hold values from -0.25 to 0.25
- dilations: int32 [2], replicated, may hold values from 1 to 8, as said below
- cotangent: bfloat16 [64, 512, 2048], P(None, 'row', 'col'), may hold values from -6 to 6
Outputs:
- pair_out: bfloat16 [64, 512, 2048], P(None, 'row', 'col')
- grad_row_features: float32 [512, 256], P(('row', 'col'))
- grad_col_features: float32 [2048, 256], P(('col', 'row'))
- grad_row_proj: float32 [256, 64], replicated
- grad_col_proj: float32 [256, 64], replicated
- grad_pair_weight: float32 [2, 3, 3, 64, 64], replicated
- grad_pair_bias: float32 [64], replicated
- grad_conv_weight: float32 [3, 3, 64, 64], replicated
Inputs may be any that keep to these rules, and one draw needn't show every extreme that they name: One of the two dilations equals 8.
All inputs are finite; a program needn't handle non-finite values.
Results may differ from a plain program's by a relative error of at most 0.0054.
Values may be sent and summed in bfloat16 or wider, within the bound.
A program may use at most 64 MiB of HBM per device.

v0:
```python
import jax
import jax.numpy as jnp
from jax import lax
from jax.sharding import PartitionSpec as P

MAX_DILATION = 8


def sent_to_all(value, axis):
    copies = jnp.broadcast_to(value, (lax.axis_size(axis), *value.shape))
    return lax.all_to_all(copies, axis, split_axis=0, concat_axis=0, tiled=True)


def in_order(tiles, dim):
    dims = list(tiles.shape[1:])
    dims[dim] *= tiles.shape[0]
    return jnp.moveaxis(tiles, 0, dim).reshape(dims)


def gathered_copies(value, axis, dim):
    tiles = sent_to_all(value, axis)
    return in_order(tiles, dim)


def padded_2(value, sides, width):
    for axis, dim in sides:
        devices, length = (lax.axis_size(axis), value.shape[dim])
        up = [(i, (i + 1) % devices) for i in range(devices - 1)]
        down = [(j, i) for i, j in up]
        last = lax.slice_in_dim(value, length - width, length, axis=dim)
        leading = lax.slice_in_dim(value, 0, width, axis=dim)
        before = lax.ppermute(last, axis, up)
        after = lax.ppermute(leading, axis, down)
        value = jnp.concatenate([before, value, after], axis=dim)
    return value


def over_copies(value, axis):
    everything = sent_to_all(value, axis)
    return jnp.sum(everything, axis=0)


def total_of_pieces(value, axis):
    tiles = lax.all_gather(value, axis)
    return tiles.sum(axis=0)


def project(features, weight):
    return jnp.dot(features, weight, preferred_element_type=jnp.float32).astype(jnp.bfloat16)


def line_terms(padded, weights, dilation, count, offset):
    shifted = jnp.stack(
        [
            lax.dynamic_slice_in_dim(padded, offset + (tap_idx - 1) * dilation, count, 0)
            for tap_idx in range(3)
        ]
    )
    return jnp.einsum("kip,kqpo->qio", shifted, weights, preferred_element_type=jnp.float32)


def line_valid(first_cell, count, cell_limit, dilation):
    cells = first_cell + jnp.arange(count, dtype=jnp.int32)
    columns = [
        (cells + (tap_idx - 1) * dilation >= 0) & (cells + (tap_idx - 1) * dilation < cell_limit)
        for tap_idx in range(3)
    ]
    return jnp.stack(columns, axis=1).astype(jnp.float32)


def inside_mask(first_cell, count, cell_limit):
    cells = first_cell + jnp.arange(count, dtype=jnp.int32)
    return ((cells >= 0) & (cells < cell_limit)).astype(jnp.float32)


def pair_field(row_terms, col_terms, row_valid, col_valid, bias):
    from_rows = jnp.einsum("jq,qic->cij", col_valid, row_terms, precision=lax.Precision.HIGHEST)
    from_cols = jnp.einsum("ik,kjc->cij", row_valid, col_terms, precision=lax.Precision.HIGHEST)
    return from_rows + from_cols + bias[:, None, None]


def window_at(padded, row_index, col_index, rows, cols):
    anchor = jnp.zeros((), jnp.int32)
    return lax.dynamic_slice(padded, (anchor, row_index, col_index), (padded.shape[0], rows, cols))


def conv_taps(padded, weight, dilation, rows, cols, margin):
    result = jnp.zeros((weight.shape[3], rows, cols), jnp.float32)
    for tap_row in range(3):
        for tap_col in range(3):
            window = window_at(
                padded,
                margin + (tap_row - 1) * dilation,
                margin + (tap_col - 1) * dilation,
                rows,
                cols,
            )
            result = result + jnp.einsum(
                "co,cij->oij", weight[tap_row, tap_col], window, preferred_element_type=jnp.float32
            )
    return result


def back_taps(padded, weight, dilation, rows, cols, margin):
    result = jnp.zeros((weight.shape[2], rows, cols), jnp.float32)
    for tap_row in range(3):
        for tap_col in range(3):
            window = window_at(
                padded,
                margin - (tap_row - 1) * dilation,
                margin - (tap_col - 1) * dilation,
                rows,
                cols,
            )
            result = result + jnp.einsum(
                "co,oij->cij", weight[tap_row, tap_col], window, preferred_element_type=jnp.float32
            )
    return result


def tap_grads(hidden_pad, grads, dilation, rows, cols, margin):
    stacked = []
    for tap_row in range(3):
        line_list = []
        for tap_col in range(3):
            window = window_at(
                hidden_pad,
                margin + (tap_row - 1) * dilation,
                margin + (tap_col - 1) * dilation,
                rows,
                cols,
            )
            line_list.append(
                jnp.einsum("cij,oij->co", window, grads, preferred_element_type=jnp.float32)
            )
        stacked.append(jnp.stack(line_list))
    return jnp.stack(stacked)


def shards(
    row_features,
    col_features,
    row_proj,
    col_proj,
    pair_weight,
    pair_bias,
    conv_weight,
    dilations,
    cotangent,
):
    first_rate = dilations[0]
    second_rate = dilations[1]
    margin = MAX_DILATION
    row_count = lax.axis_size("row")
    col_count = lax.axis_size("col")
    row_place = lax.axis_index("row")
    col_place = lax.axis_index("col")
    rows_here = cotangent.shape[1]
    cols_here = cotangent.shape[2]
    row_start = row_place * rows_here
    col_start = col_place * cols_here
    row_limit = rows_here * row_count
    col_limit = cols_here * col_count
    row_piece = row_features.shape[0]
    col_piece = col_features.shape[0]
    rows_a = gathered_copies(project(row_features, row_proj), "col", 0)
    cols_b = gathered_copies(project(col_features, col_proj), "row", 0)
    pad_reach = 2 * margin
    a_pad = padded_2(rows_a, (("row", 0),), 2 * MAX_DILATION)
    b_pad = padded_2(cols_b, (("col", 0),), 2 * MAX_DILATION)
    row_terms = line_terms(
        a_pad, pair_weight[0], first_rate, rows_here + 2 * margin, pad_reach - margin
    )
    col_terms = line_terms(
        b_pad,
        jnp.swapaxes(pair_weight[1], 0, 1),
        first_rate,
        cols_here + 2 * margin,
        pad_reach - margin,
    )
    row_valid = line_valid(row_start - margin, rows_here + 2 * margin, row_limit, first_rate)
    col_valid = line_valid(col_start - margin, cols_here + 2 * margin, col_limit, first_rate)
    pre_act = pair_field(row_terms, col_terms, row_valid, col_valid, pair_bias)
    row_inside = inside_mask(row_start - margin, rows_here + 2 * margin, row_limit)
    col_inside = inside_mask(col_start - margin, cols_here + 2 * margin, col_limit)
    hidden = (jax.nn.silu(pre_act) * row_inside[None, :, None] * col_inside[None, None, :]).astype(
        jnp.bfloat16
    )
    pre_own = pre_act[:, margin : margin + rows_here, margin : margin + cols_here]
    hidden_own = hidden[:, margin : margin + rows_here, margin : margin + cols_here]
    conv_mixed = conv_taps(hidden, conv_weight, second_rate, rows_here, cols_here, margin)
    pair_out = (hidden_own.astype(jnp.float32) + conv_mixed).astype(jnp.bfloat16)
    grad_pad = padded_2(cotangent, (("row", 1), ("col", 2)), MAX_DILATION)
    d_hidden = cotangent.astype(jnp.float32) + back_taps(
        grad_pad, conv_weight, second_rate, rows_here, cols_here, margin
    )
    conv_grad = tap_grads(hidden, cotangent, second_rate, rows_here, cols_here, margin)
    sigmoid_own = jax.nn.sigmoid(pre_own)
    d_pre = d_hidden * sigmoid_own * (1.0 + pre_own * (1.0 - sigmoid_own))
    bias_grad = jnp.sum(d_pre, axis=(1, 2))
    row_valid_own = line_valid(row_start, rows_here, row_limit, first_rate)
    col_valid_own = line_valid(col_start, cols_here, col_limit, first_rate)
    row_part = jnp.einsum("jq,cij->qic", col_valid_own, d_pre, precision=lax.Precision.HIGHEST)
    col_part = jnp.einsum("ik,cij->kjc", row_valid_own, d_pre, precision=lax.Precision.HIGHEST)
    row_sums = over_copies(row_part, "col")
    col_sums = total_of_pieces(col_part, "row")
    back_rows = jnp.einsum(
        "qio,kqpo->kip",
        row_sums,
        pair_weight[0].astype(jnp.float32),
        precision=lax.Precision.HIGHEST,
    )
    back_cols = jnp.einsum(
        "kjo,kqpo->qjp",
        col_sums,
        pair_weight[1].astype(jnp.float32),
        precision=lax.Precision.HIGHEST,
    )
    rows_back_pad = padded_2(back_rows, (("row", 1),), MAX_DILATION)
    cols_back_pad = padded_2(back_cols, (("col", 1),), MAX_DILATION)
    row_own = col_place * row_piece
    col_own = row_place * col_piece
    d_rows = sum(
        (
            lax.dynamic_slice_in_dim(
                rows_back_pad[tap_idx], margin + row_own - (tap_idx - 1) * first_rate, row_piece, 0
            )
            for tap_idx in range(3)
        )
    )
    d_cols = sum(
        (
            lax.dynamic_slice_in_dim(
                cols_back_pad[tap_idx], margin + col_own - (tap_idx - 1) * first_rate, col_piece, 0
            )
            for tap_idx in range(3)
        )
    )
    d_rows = d_rows.astype(jnp.bfloat16)
    d_cols = d_cols.astype(jnp.bfloat16)
    grad_row_features = jnp.dot(d_rows, row_proj.T, preferred_element_type=jnp.float32)
    grad_col_features = jnp.dot(d_cols, col_proj.T, preferred_element_type=jnp.float32)
    grad_row_proj = jnp.dot(row_features.T, d_rows, preferred_element_type=jnp.float32)
    grad_col_proj = jnp.dot(col_features.T, d_cols, preferred_element_type=jnp.float32)
    row_shifted = jnp.stack(
        [
            lax.dynamic_slice_in_dim(
                a_pad, pad_reach + row_own + (tap_idx - 1) * first_rate, row_piece, 0
            )
            for tap_idx in range(3)
        ]
    )
    col_shifted = jnp.stack(
        [
            lax.dynamic_slice_in_dim(
                b_pad, pad_reach + col_own + (tap_idx - 1) * first_rate, col_piece, 0
            )
            for tap_idx in range(3)
        ]
    )
    row_sums_own = lax.dynamic_slice_in_dim(row_sums, row_own, row_piece, 1)
    col_sums_own = lax.dynamic_slice_in_dim(col_sums, col_own, col_piece, 1)
    grad_row_pair = jnp.einsum(
        "kip,qio->kqpo",
        row_shifted.astype(jnp.float32),
        row_sums_own,
        precision=lax.Precision.HIGHEST,
    )
    grad_col_pair = jnp.einsum(
        "qjp,kjo->kqpo",
        col_shifted.astype(jnp.float32),
        col_sums_own,
        precision=lax.Precision.HIGHEST,
    )
    summed = lax.psum(
        (
            grad_row_proj,
            grad_col_proj,
            jnp.stack([grad_row_pair, grad_col_pair]),
            bias_grad,
            conv_grad,
        ),
        ("row", "col"),
    )
    return (
        pair_out,
        grad_row_features,
        grad_col_features,
        summed[0],
        summed[1],
        summed[2],
        summed[3],
        summed[4],
    )


def solution(mesh):
    return jax.shard_map(
        shards,
        mesh=mesh,
        in_specs=(
            P(("row", "col"), None),
            P(("col", "row"), None),
            P(),
            P(),
            P(),
            P(),
            P(),
            P(),
            P(None, "row", "col"),
        ),
        out_specs=(
            P(None, "row", "col"),
            P(("row", "col"), None),
            P(("col", "row"), None),
            P(),
            P(),
            P(),
            P(),
            P(),
        ),
        check_vma=False,
    )
```

profile of v0, /device:TPU:8, one launch (start us, length us, event | category | flops | bytes accessed | tf_op | source)
XLA Modules:
  0.0 497.2 jit_solution(1693750690878822578)
XLA Ops:
  7.2 1.0 convolution_convert_fusion.1
  8.2 0.6 broadcast_in_dim.12
  8.8 6.3 %all-to-all-start = ((bf16[8,2,64]{2,1,0:T(2,128)(2,1)}), bf16[8,2,64]{2,1,0:T(2,128)(2,1)S(1)}, u32[]{:S(2)}, u32[]{:S(2)}) async-start(bf16[8,2,64]{2,1,0:T(2,128)(2,1)} %broadcast_in_dim.12), calls=%async_computation | async-start | bytes 8192 | tf_op jit(solution)/shard_map/all_to_all | solution.py:11
  15.1 1.1 fusion.201
  16.2 1.3 collective-permute-start.4
  17.6 1.3 collective-permute-start.5
  18.9 0.6 fusion.207
  20.1 0.7 compare_and_fusion.9
  20.8 1.2 compare_and_fusion
  22.0 0.5 and_convert_fusion
  22.6 0.7 compare_and_fusion.6
  23.3 1.0 fusion.73
  24.4 0.6 compare_and_fusion.8
  25.0 0.7 reshape.293
  25.7 15.1 %all-to-all-start.1 = ((bf16[32,2,256]{2,1,0:T(2,128)(2,1)}), bf16[32,2,256]{2,1,0:T(2,128)(2,1)S(1)}, u32[]{:S(2)}, u32[]{:S(2)}) async-start(bf16[32,2,256]{2,1,0:T(2,128)(2,1)} %reshape.293), calls=%async_computation.1 | async-start | bytes 65536 | tf_op jit(solution)/shard_map/all_to_all | solution.py:11
  40.9 2.2 collective-permute-start
  43.1 1.3 collective-permute-start.1
  49.2 1.5 all-to-all-done.1
  51.0 3.3 collective-permute-start.2
  54.4 3.4 collective-permute-start.3
  57.8 0.8 convolution_bitcast_fusion.11
  58.7 1.3 collective-permute-done.3
  60.5 1.5 fusion.46
  62.6 4.3 collective-permute-start.6
  66.9 2.6 collective-permute-start.7
  69.5 4.6 multiply_convert_fusion
  74.2 6.0 %collective-permute-done.6 = bf16[64,32,8]{2,0,1:T(8,128)(2,1)S(1)} collective-permute-done((bf16[64,32,8]{2,0,1:T(8,128)(2,1)S(1)}, bf16[64,32,8]{2,0,1:T(8,128)(2,1)S(1)}, u32[]{:S(2)}, u32[]{:S(2)}) %collective-permute-start.6) | collective-permute-done | bytes 32800 | tf_op jit(solution)/shard_map/ppermute | solution.py:32
  80.2 9.6 %collective-permute-done.7 = bf16[64,32,8]{2,0,1:T(8,128)(2,1)S(1)} collective-permute-done((bf16[64,32,8]{2,0,1:T(8,128)(2,1)S(1)}, bf16[64,32,8]{2,0,1:T(8,128)(2,1)S(1)}, u32[]{:S(2)}, u32[]{:S(2)}) %collective-permute-start.7) | collective-permute-done | bytes 32800 | tf_op jit(solution)/shard_map/ppermute | solution.py:33
  89.8 1.1 pad_maximum_fusion
  93.1 0.5 fusion.11
  93.7 1.8 fusion.208
  95.4 1.1 convolution_bitcast_fusion.7
  96.5 0.7 copy.231
  101.8 0.7 compare_and_fusion.3
  102.5 0.5 fusion.174
  104.4 0.6 maximum_bitcast_fusion.2
  105.5 0.7 convolution_bitcast_fusion.12
  106.6 0.7 maximum_bitcast_fusion.4
  107.7 1.1 convolution_bitcast_fusion.15
  109.2 1.1 convolution_bitcast_fusion.16
  113.6 0.7 convolution_bitcast_fusion.21
  114.3 0.8 reshape.295
  115.2 4.9 all-to-all-start.2
  120.2 0.7 pad_maximum_fusion.3
  120.9 4.6 all-to-all-done.2
  126.0 0.9 reduce
  127.3 1.3 collective-permute-start.8
  128.6 1.3 collective-permute-start.9
  130.2 1.1 copy.246
  131.3 81.3 %psum.38 = f32[64]{0:T(128)} all-reduce(f32[64]{0:T(128)S(1)} %copy-done.22), channel_id=1, replica_groups=mesh['row'=32,'col'=8] {'row','col'}, use_global_device_ids=true, to_apply=%region_6.7 | all-reduce | flops 64 | bytes 512 | tf_op jit(solution)/shard_map/psum | solution.py:275
  213.1 0.8 convolution_bitcast_fusion.10
  213.9 3.2 reduce_sum.28
  217.5 3.2 collective-permute-start.10
  220.7 3.5 collective-permute-start.11
  224.6 0.9 pad_maximum_fusion.1
  225.5 1.8 collective-permute-done.11
  227.6 0.8 convolution_bitcast_fusion.9
  228.3 0.7 fusion.178
  229.1 0.8 fusion.211
  229.8 254.7 %all-reduce.3.cloned.1.call-done = (f32[256,64]{0,1:T(8,128)}, f32[256,64]{0,1:T(8,128)}, f32[2,3,3,64,64]{3,4,1,2,0:T(8,128)}, f32[3,3,64,64]{3,2,1,0:T(8,128)}) async-done(((f32[256,64]{0,1:T(8,128)}, f32[256,64]{0,1:T(8,128)}, f32[2,3,3,64,64]{3,4,1,2,0:T(8,128)}, f32[3,3,64,64]{3,2,1,0:T(8,128)}), (f32[256,64]{0,1:T(8,128)}, f32[256,64]{0,1:T(8,128)}, f32[2,3,3,64,64]{3,4,1,2,0:T(8,128)}, ...) | async-done | bytes 573456 | tf_op jit(solution)/shard_map/psum | solution.py:275
  484.5 2.1 copy.247
  486.7 1.5 copy.329
  488.2 1.5 copy.330
  489.6 0.7 copy.331
  (128 shorter events, 13.2 us)
Async XLA Ops:
  7.2 17.1 %copy-start = (bf16[256,64]{0,1:T(8,128)(2,1)S(1)}, bf16[256,64]{0,1:T(8,128)(2,1)}, u32[]{:S(2)}) copy-start(bf16[256,64]{0,1:T(8,128)(2,1)} %param.12) | copy-start | bytes 98308
  7.2 16.1 %copy-start.1 = (bf16[64,16,256]{2,1,0:T(8,128)(2,1)S(1)}, bf16[64,16,256]{2,1,0:T(8,128)(2,1)}, u32[]{:S(2)}) copy-start(bf16[64,16,256]{2,1,0:T(8,128)(2,1)} %param.17) | copy-start | bytes 1572868
  7.2 11.7 %copy-start.16 = (s32[2]{0:T(128)S(1)}, s32[2]{0:T(128)}, u32[]{:S(2)}) copy-start(s32[2]{0:T(128)} %param.16) | copy-start | bytes 28
  7.2 16.0 %copy-start.2 = (bf16[2,3,3,64,64]{4,3,2,1,0:T(8,128)(2,1)S(1)}, bf16[2,3,3,64,64]{4,3,2,1,0:T(8,128)(2,1)}, u32[]{:S(2)}) copy-start(bf16[2,3,3,64,64]{4,3,2,1,0:T(8,128)(2,1)} %param.13) | copy-start | bytes 442372
  8.8 16.9 %all-to-all-start = ((bf16[8,2,64]{2,1,0:T(2,128)(2,1)}), bf16[8,2,64]{2,1,0:T(2,128)(2,1)S(1)}, u32[]{:S(2)}, u32[]{:S(2)}) async-start(bf16[8,2,64]{2,1,0:T(2,128)(2,1)} %broadcast_in_dim.12), calls=%async_computation | async-start | bytes 8192 | tf_op jit(solution)/shard_map/all_to_all | solution.py:11
  16.1 8.2 %copy-start.11 = (bf16[8,256]{1,0:T(8,128)(2,1)S(1)}, bf16[8,256]{1,0:T(8,128)(2,1)}, u32[]{:S(2)}) copy-start(bf16[8,256]{1,0:T(8,128)(2,1)} %param.10) | copy-start | bytes 12292
  16.2 45.8 %collective-permute-start.4 = (bf16[64,8,256]{2,0,1:T(8,128)(2,1)S(1)}, bf16[64,8,256]{2,0,1:T(8,128)(2,1)S(1)}, u32[]{:S(2)}, u32[]{:S(2)}) collective-permute-start(bf16[64,8,256]{2,0,1:T(8,128)(2,1)S(1)} %copy.319), channel_id=1, source_target_pairs={{0,8},{8,16},{16,24},{24,32},{32,40},{40,48},{48,56},{56,64},{64,7... | collective-permute-start | bytes 786440 | tf_op jit(solution)/shard_map/ppermute | solution.py:32
  17.6 44.7 %collective-permute-start.5 = (bf16[64,8,256]{2,0,1:T(8,128)(2,1)S(1)}, bf16[64,8,256]{2,0,1:T(8,128)(2,1)S(1)}, u32[]{:S(2)}, u32[]{:S(2)}) collective-permute-start(bf16[64,8,256]{2,0,1:T(8,128)(2,1)S(1)} %copy.320), channel_id=1, source_target_pairs={{8,0},{16,8},{24,16},{32,24},{40,32},{48,40},{56,48},{64,56},{72,6... | collective-permute-start | bytes 786440 | tf_op jit(solution)/shard_map/ppermute | solution.py:33
  25.7 25.0 %all-to-all-start.1 = ((bf16[32,2,256]{2,1,0:T(2,128)(2,1)}), bf16[32,2,256]{2,1,0:T(2,128)(2,1)S(1)}, u32[]{:S(2)}, u32[]{:S(2)}) async-start(bf16[32,2,256]{2,1,0:T(2,128)(2,1)} %reshape.293), calls=%async_computation.1 | async-start | bytes 65536 | tf_op jit(solution)/shard_map/all_to_all | solution.py:11
  40.9 173.0 %all-gather.3.cloned.1.call-start = ((), (), s32[]{:S(2)}) async-start(), calls=%async_computation.3 | async-start | bytes 6488064 | tf_op jit(solution)/shard_map/all_gather | solution.py:44
  40.9 8.2 %collective-permute-start = (bf16[16,64]{1,0:T(8,128)(2,1)S(1)}, bf16[16,64]{1,0:T(8,128)(2,1)S(1)}, u32[]{:S(2)}, u32[]{:S(2)}) collective-permute-start(bf16[16,64]{1,0:T(8,128)(2,1)S(1)} %bitcast.322), channel_id=1, source_target_pairs={{0,8},{8,16},{16,24},{24,32},{32,40},{40,48},{48,56},{56,64},{64,7... | collective-permute-start | bytes 6152 | tf_op jit(solution)/shard_map/ppermute | solution.py:32
  43.1 6.0 %collective-permute-start.1 = (bf16[16,64]{1,0:T(8,128)(2,1)S(1)}, bf16[16,64]{1,0:T(8,128)(2,1)S(1)}, u32[]{:S(2)}, u32[]{:S(2)}) collective-permute-start(bf16[16,64]{1,0:T(8,128)(2,1)S(1)} %bitcast.323), channel_id=1, source_target_pairs={{8,0},{16,8},{24,16},{32,24},{40,32},{48,40},{56,48},{64,56},{72,6... | collective-permute-start | bytes 6152 | tf_op jit(solution)/shard_map/ppermute | solution.py:33
  51.0 7.8 %collective-permute-start.2 = (bf16[16,64]{0,1:T(8,128)(2,1)S(1)}, bf16[16,64]{0,1:T(8,128)(2,1)S(1)}, u32[]{:S(2)}, u32[]{:S(2)}) collective-permute-start(bf16[16,64]{0,1:T(8,128)(2,1)S(1)} %copy.199), channel_id=1, source_target_pairs={{0,1},{1,2},{2,3},{3,4},{4,5},{5,6},{6,7},{8,9},{9,10},{10,11},{11... | collective-permute-start | bytes 6152 | tf_op jit(solution)/shard_map/ppermute | solution.py:32
  54.4 5.6 %collective-permute-start.3 = (bf16[16,64]{0,1:T(8,128)(2,1)S(1)}, bf16[16,64]{0,1:T(8,128)(2,1)S(1)}, u32[]{:S(2)}, u32[]{:S(2)}) collective-permute-start(bf16[16,64]{0,1:T(8,128)(2,1)S(1)} %copy.200), channel_id=1, source_target_pairs={{1,0},{2,1},{3,2},{4,3},{5,4},{6,5},{7,6},{9,8},{10,9},{11,10},{12... | collective-permute-start | bytes 6152 | tf_op jit(solution)/shard_map/ppermute | solution.py:33
  62.2 7.3 %copy-start.17 = (pred[272,1]{0,1:T(4,128)(4,1)S(1)}, pred[272,1]{0,1:T(4,128)(4,1)}, u32[]{:S(2)}) copy-start(pred[272,1]{0,1:T(4,128)(4,1)} %get-tuple-element.89) | copy-start | bytes 820
  62.2 7.3 %copy-start.20 = (f32[64]{0:T(128)S(1)}, f32[64]{0:T(128)}, u32[]{:S(2)}) copy-start(f32[64]{0:T(128)} %param.14) | copy-start | bytes 772
  62.2 7.3 %copy-start.21 = (f32[3,32,64]{2,1,0:T(8,128)S(1)}, f32[3,32,64]{2,1,0:T(8,128)}, u32[]{:S(2)}) copy-start(f32[3,32,64]{2,1,0:T(8,128)} %convolution_bitcast_fusion.11) | copy-start | bytes 73732
  62.2 7.3 %copy-start.23 = (f32[32]{0:T(128)S(1)}, f32[32]{0:T(128)}, u32[]{:S(2)}) copy-start(f32[32]{0:T(128)} %and_convert_fusion) | copy-start | bytes 388
  62.6 17.7 %collective-permute-start.6 = (bf16[64,32,8]{2,0,1:T(8,128)(2,1)S(1)}, bf16[64,32,8]{2,0,1:T(8,128)(2,1)S(1)}, u32[]{:S(2)}, u32[]{:S(2)}) collective-permute-start(bf16[64,32,8]{2,0,1:T(8,128)(2,1)S(1)} %get-tuple-element.52), channel_id=1, source_target_pairs={{0,1},{1,2},{2,3},{3,4},{4,5},{5,6},{6,7},{8,9},{9,10},{10,11},{11... | collective-permute-start | bytes 98312 | tf_op jit(solution)/shard_map/ppermute | solution.py:32
  66.9 22.9 %collective-permute-start.7 = (bf16[64,32,8]{2,0,1:T(8,128)(2,1)S(1)}, bf16[64,32,8]{2,0,1:T(8,128)(2,1)S(1)}, u32[]{:S(2)}, u32[]{:S(2)}) collective-permute-start(bf16[64,32,8]{2,0,1:T(8,128)(2,1)S(1)} %get-tuple-element.53), channel_id=1, source_target_pairs={{1,0},{2,1},{3,2},{4,3},{5,4},{6,5},{7,6},{9,8},{10,9},{11,10},{12... | collective-permute-start | bytes 98312 | tf_op jit(solution)/shard_map/ppermute | solution.py:33
  74.2 16.7 %copy-start.3 = (bf16[3,3,64,64]{3,2,1,0:T(8,128)(2,1)S(1)}, bf16[3,3,64,64]{3,2,1,0:T(8,128)(2,1)}, u32[]{:S(2)}) copy-start(bf16[3,3,64,64]{3,2,1,0:T(8,128)(2,1)} %param.15) | copy-start | bytes 221188
  93.6 1.8 copy-start.19
  106.2 2.6 copy-start.4
  113.5 6.6 %copy-start.9 = (f32[1,64,64]{2,1,0:T(8,128)S(1)}, f32[1,64,64]{2,1,0:T(8,128)}, u32[]{:S(2)}) copy-start(f32[1,64,64]{2,1,0:T(8,128)} %convolution_bitcast_fusion.15) | copy-start | bytes 49156
  113.5 6.6 %copy-start.10 = (f32[1,64,64]{2,1,0:T(8,128)S(1)}, f32[1,64,64]{2,1,0:T(8,128)}, u32[]{:S(2)}) copy-start(f32[1,64,64]{2,1,0:T(8,128)} %convolution_bitcast_fusion.16) | copy-start | bytes 49156
  113.5 6.6 %copy-start.5 = (f32[1,3,64,64]{3,2,1,0:T(8,128)S(1)}, f32[1,3,64,64]{3,2,1,0:T(8,128)}, u32[]{:S(2)}) copy-start(f32[1,3,64,64]{3,2,1,0:T(8,128)} %maximum_bitcast_fusion.2) | copy-start | bytes 147460
  113.6 6.6 %copy-start.6 = (f32[1,3,64,64]{3,2,1,0:T(8,128)S(1)}, f32[1,3,64,64]{3,2,1,0:T(8,128)}, u32[]{:S(2)}) copy-start(f32[1,3,64,64]{3,2,1,0:T(8,128)} %maximum_bitcast_fusion.4) | copy-start | bytes 147460
  115.1 16.2 %copy-start.22 = (f32[64]{0:T(128)S(1)}, f32[64]{0:T(128)}, u32[]{:S(2)}) copy-start(f32[64]{0:T(128)} %get-tuple-element.86) | copy-start | bytes 772
  115.1 97.5 %copy-start.13 = (bf16[1,2,64]{2,1,0:T(2,128)(2,1)S(1)}, bf16[1,2,64]{2,1,0:T(2,128)(2,1)}, u32[]{:S(2)}) copy-start(bf16[1,2,64]{2,1,0:T(2,128)(2,1)} %get-tuple-element.76) | copy-start | bytes 772
  115.1 97.5 %copy-start.14 = (bf16[1,2,64]{2,1,0:T(2,128)(2,1)S(1)}, bf16[1,2,64]{2,1,0:T(2,128)(2,1)}, u32[]{:S(2)}) copy-start(bf16[1,2,64]{2,1,0:T(2,128)(2,1)} %get-tuple-element.77) | copy-start | bytes 772
  115.1 97.5 %copy-start.15 = (bf16[1,2,64]{2,1,0:T(2,128)(2,1)S(1)}, bf16[1,2,64]{2,1,0:T(2,128)(2,1)}, u32[]{:S(2)}) copy-start(bf16[1,2,64]{2,1,0:T(2,128)(2,1)} %get-tuple-element.78) | copy-start | bytes 772
  115.2 10.3 %all-to-all-start.2 = ((f32[8,1,3072]{2,1,0:T(1,128)}), f32[8,1,3072]{2,1,0:T(1,128)S(1)}, u32[]{:S(2)}, u32[]{:S(2)}) async-start(f32[8,1,3072]{2,1,0:T(1,128)} %reshape.295), calls=%async_computation.2 | async-start | bytes 196608 | tf_op jit(solution)/shard_map/all_to_all | solution.py:11
  120.1 364.5 %all-reduce.3.cloned.1.call-start = ((), (), s32[]{:S(2)}) async-start(), calls=%async_computation.4 | async-start | bytes 2031616 | tf_op jit(solution)/shard_map/psum | solution.py:275
  120.1 92.9 %copy-start.18 = (bf16[2,256]{1,0:T(2,128)(2,1)S(1)}, bf16[2,256]{1,0:T(2,128)(2,1)}, u32[]{:S(2)}) copy-start(bf16[2,256]{1,0:T(2,128)(2,1)} %param.9) | copy-start | bytes 3076
  127.3 85.7 %collective-permute-start.8 = (f32[3,8,64]{2,1,0:T(8,128)S(1)}, f32[3,8,64]{2,1,0:T(8,128)S(1)}, u32[]{:S(2)}, u32[]{:S(2)}) collective-permute-start(f32[3,8,64]{2,1,0:T(8,128)S(1)} %get-tuple-element.74), channel_id=1, source_target_pairs={{0,8},{8,16},{16,24},{24,32},{32,40},{40,48},{48,56},{56,64},{64,7... | collective-permute-start | bytes 18440 | tf_op jit(solution)/shard_map/ppermute | solution.py:32
  128.6 84.4 %collective-permute-start.9 = (f32[3,8,64]{2,1,0:T(8,128)S(1)}, f32[3,8,64]{2,1,0:T(8,128)S(1)}, u32[]{:S(2)}, u32[]{:S(2)}) collective-permute-start(f32[3,8,64]{2,1,0:T(8,128)S(1)} %get-tuple-element.75), channel_id=1, source_target_pairs={{8,0},{16,8},{24,16},{32,24},{40,32},{48,40},{56,48},{64,56},{72,6... | collective-permute-start | bytes 18440 | tf_op jit(solution)/shard_map/ppermute | solution.py:33
  217.5 10.1 %copy-start.12 = (bf16[8,256]{1,0:T(8,128)(2,1)S(1)}, bf16[8,256]{1,0:T(8,128)(2,1)}, u32[]{:S(2)}) copy-start(bf16[8,256]{1,0:T(8,128)(2,1)} %param.10) | copy-start | bytes 12292
  217.5 8.0 %collective-permute-start.10 = (f32[3,8,64]{1,2,0:T(8,128)S(1)}, f32[3,8,64]{1,2,0:T(8,128)S(1)}, u32[]{:S(2)}, u32[]{:S(2)}) collective-permute-start(f32[3,8,64]{1,2,0:T(8,128)S(1)} %get-tuple-element.61), channel_id=1, source_target_pairs={{0,1},{1,2},{2,3},{3,4},{4,5},{5,6},{6,7},{8,9},{9,10},{10,11},{11... | collective-permute-start | bytes 18440 | tf_op jit(solution)/shard_map/ppermute | solution.py:32
  220.7 6.5 %collective-permute-start.11 = (f32[3,8,64]{1,2,0:T(8,128)S(1)}, f32[3,8,64]{1,2,0:T(8,128)S(1)}, u32[]{:S(2)}, u32[]{:S(2)}) collective-permute-start(f32[3,8,64]{1,2,0:T(8,128)S(1)} %get-tuple-element.62), channel_id=1, source_target_pairs={{1,0},{2,1},{3,2},{4,3},{5,4},{6,5},{7,6},{9,8},{10,9},{11,10},{12... | collective-permute-start | bytes 18440 | tf_op jit(solution)/shard_map/ppermute | solution.py:33
  224.6 3.7 copy-start.8
  484.5 5.1 %copy-start.7 = (f32[3,3,64,64]{3,2,1,0:T(8,128)S(1)}, f32[3,3,64,64]{3,2,1,0:T(8,128)}, u32[]{:S(2)}) copy-start(f32[3,3,64,64]{3,2,1,0:T(8,128)} %get-tuple-element.103) | copy-start | bytes 442372
Sparse Core Ops, SparseCore 0:
  97.3 69.7 all-gather.2
  228.5 256.0 all-reduce.2
where the time goes:
time: 498 us; the launch traced here: 497 us
  waiting for transfers between devices  280 us (56%)
  blocking collectives  81.3 us (16%)
  starting transfers between devices  55.4 us (11%)
  matrix products  29 us (6%)
  between operations  24.8 us (5%)
  local copies, waits for them, and re-layouts  14.5 us (3%)
  other arithmetic  12.7 us (3%)
    psum x1, waiting for transfers between devices, shards(): lax.psum((grad_row_proj, grad_col_proj, jnp.stack([grad_row_pair, grad_co...  255 us
    psum x1, blocking collectives, shards(): lax.psum((grad_row_proj, grad_col_proj, jnp.stack([grad_row_pair, grad_co...  81.3 us
    all_to_all x3, starting transfers between devices, sent_to_all(): return lax.all_to_all(copies, axis, split_axis=0, concat_axis=0, tiled=True)  26.3 us
    ppermute x6, starting transfers between devices, padded_2(): before = lax.ppermute(last, axis, up)  15.6 us
    ppermute x6, starting transfers between devices, padded_2(): after = lax.ppermute(leading, axis, down)  13.4 us
    ppermute x6, waiting for transfers between devices, padded_2(): after = lax.ppermute(leading, axis, down)  12.6 us
  transfers between devices with their start and end apart: 17, of which 7 were waited for; matrix products, arithmetic and copies ran while one was open for 7% of the time, Pallas kernels for 0%

commit v1 on v0

--- a/solution.py
+++ b/solution.py
@@ -273,14 +273,17 @@
         precision=lax.Precision.HIGHEST,
     )
     summed = lax.psum(
-        (
-            grad_row_proj,
-            grad_col_proj,
-            jnp.stack([grad_row_pair, grad_col_pair]),
-            bias_grad,
-            conv_grad,
+        lax.psum(
+            (
+                grad_row_proj,
+                grad_col_proj,
+                jnp.stack([grad_row_pair, grad_col_pair]),
+                bias_grad,
+                conv_grad,
+            ),
+            "col",
         ),
-        ("row", "col"),
+        "row",
     )
     return (
         pair_out,

time: 498 us -> 570 us (1.14)
  waiting for transfers between devices: 280 us -> 341 us
  blocking collectives: 81.3 us -> 87.5 us
    psum x0 -> x1, waiting for transfers between devices: none -> 199 us  [shards(): lax.psum(lax.psum((grad_row_proj, grad_col_proj, jnp.stack([grad_row_pair...]
    psum x1, waiting for transfers between devices: 255 us -> 79.8 us  [shards(): lax.psum((grad_row_proj, grad_col_proj, jnp.stack([grad_row_pair, grad_co...]
    psum x0 -> x1, blocking collectives: none -> 70.4 us  [shards(): lax.psum(lax.psum((grad_row_proj, grad_col_proj, jnp.stack([grad_row_pair...]
    psum x1, blocking collectives: 81.3 us -> 17.1 us  [shards(): lax.psum((grad_row_proj, grad_col_proj, jnp.stack([grad_row_pair, grad_co...]
    all_gather x1, waiting for transfers between devices: 0.01 us -> 34 us  [total_of_pieces(): tiles = lax.all_gather(value, axis)]
  transfers between devices with their start and end apart: 17 -> 18, of which waited for: 7 -> 10; matrix products, arithmetic and copies ran while one was open for 7% -> 7% of each run, Pallas kernels for 0% -> 0%
where the time goes in v1:
time: 570 us; the launch traced here: 568 us
  waiting for transfers between devices  341 us (60%)
  blocking collectives  87.5 us (15%)
  starting transfers between devices  55.3 us (10%)
  matrix products  32.9 us (6%)
  between operations  24.5 us (4%)
  local copies, waits for them, and re-layouts  14.5 us (3%)
  other arithmetic  12.7 us (2%)
    psum x1, waiting for transfers between devices, shards(): lax.psum(lax.psum((grad_row_proj, grad_col_proj, jnp.stack([grad_row_pair...  199 us
    psum x1, waiting for transfers between devices, shards(): lax.psum((grad_row_proj, grad_col_proj, jnp.stack([grad_row_pair, grad_co...  79.8 us
    psum x1, blocking collectives, shards(): lax.psum(lax.psum((grad_row_proj, grad_col_proj, jnp.stack([grad_row_pair...  70.4 us
    all_gather x1, waiting for transfers between devices, total_of_pieces(): tiles = lax.all_gather(value, axis)  34 us
    all_to_all x3, starting transfers between devices, sent_to_all(): return lax.all_to_all(copies, axis, split_axis=0, concat_axis=0, tiled=True)  26.2 us
    psum x1, blocking collectives, shards(): lax.psum((grad_row_proj, grad_col_proj, jnp.stack([grad_row_pair, grad_co...  17.1 us
    ppermute x6, waiting for transfers between devices, padded_2(): after = lax.ppermute(leading, axis, down)  15.6 us
    ppermute x6, starting transfers between devices, padded_2(): after = lax.ppermute(leading, axis, down)  14.6 us
  transfers between devices with their start and end apart: 18, of which 10 were waited for; matrix products, arithmetic and copies ran while one was open for 7% of the time, Pallas kernels for 0%

profile of v1, /device:TPU:8, one launch (start us, length us, event | category | flops | bytes accessed | tf_op | source)
XLA Modules:
  0.0 568.3 jit_solution(14458506347573584178)
XLA Ops:
  7.2 1.0 convolution_convert_fusion.1
  8.8 6.3 %all-to-all-start = ((bf16[8,2,64]{2,1,0:T(2,128)(2,1)}), bf16[8,2,64]{2,1,0:T(2,128)(2,1)S(1)}, u32[]{:S(2)}, u32[]{:S(2)}) async-start(bf16[8,2,64]{2,1,0:T(2,128)(2,1)} %broadcast_in_dim.12), calls=%async_computation | async-start | bytes 8192 | tf_op jit(solution)/shard_map/all_to_all | solution.py:11
  15.1 1.1 fusion.201
  16.2 1.3 collective-permute-start.4
  17.6 1.3 collective-permute-start.5
  20.8 1.2 compare_and_fusion
  23.3 1.0 fusion.73
  25.0 0.7 reshape.293
  25.7 15.1 %all-to-all-start.1 = ((bf16[32,2,256]{2,1,0:T(2,128)(2,1)}), bf16[32,2,256]{2,1,0:T(2,128)(2,1)S(1)}, u32[]{:S(2)}, u32[]{:S(2)}) async-start(bf16[32,2,256]{2,1,0:T(2,128)(2,1)} %reshape.293), calls=%async_computation.1 | async-start | bytes 65536 | tf_op jit(solution)/shard_map/all_to_all | solution.py:11
  40.9 2.2 collective-permute-start
  43.1 1.3 collective-permute-start.1
  49.2 1.5 all-to-all-done.1
  51.0 3.3 collective-permute-start.2
  54.4 3.4 collective-permute-start.3
  57.8 0.8 convolution_bitcast_fusion.11
  58.7 1.3 collective-permute-done.3
  60.5 1.5 fusion.46
  62.6 4.3 collective-permute-start.6
  66.9 2.6 collective-permute-start.7
  69.5 4.6 multiply_convert_fusion
  74.2 6.0 %collective-permute-done.6 = bf16[64,32,8]{2,0,1:T(8,128)(2,1)S(1)} collective-permute-done((bf16[64,32,8]{2,0,1:T(8,128)(2,1)S(1)}, bf16[64,32,8]{2,0,1:T(8,128)(2,1)S(1)}, u32[]{:S(2)}, u32[]{:S(2)}) %collective-permute-start.6) | collective-permute-done | bytes 32800 | tf_op jit(solution)/shard_map/ppermute | solution.py:32
  80.2 9.6 %collective-permute-done.7 = bf16[64,32,8]{2,0,1:T(8,128)(2,1)S(1)} collective-permute-done((bf16[64,32,8]{2,0,1:T(8,128)(2,1)S(1)}, bf16[64,32,8]{2,0,1:T(8,128)(2,1)S(1)}, u32[]{:S(2)}, u32[]{:S(2)}) %collective-permute-start.7) | collective-permute-done | bytes 32800 | tf_op jit(solution)/shard_map/ppermute | solution.py:33
  89.8 1.1 pad_maximum_fusion
  93.7 1.8 fusion.208
  95.5 1.1 convolution_bitcast_fusion.7
  96.6 0.7 copy.231
  101.9 0.7 compare_and_fusion.3
  105.6 0.7 convolution_bitcast_fusion.12
  106.7 0.7 maximum_bitcast_fusion.4
  107.8 1.1 convolution_bitcast_fusion.15
  109.3 1.1 convolution_bitcast_fusion.16
  111.5 1.4 convolution_add_fusion.5
  112.9 0.7 convolution_bitcast_fusion.21
  113.7 0.8 reshape.295
  114.5 4.8 all-to-all-start.2
  119.4 0.7 pad_maximum_fusion.3
  120.1 4.3 all-to-all-done.2
  124.9 0.9 reduce
  126.3 1.3 collective-permute-start.8
  127.6 1.3 collective-permute-start.9
  129.6 2.8 collective-permute-done.9
  132.5 0.8 convolution_bitcast_fusion.10
  133.3 34.0 %all-gather.3.cloned.1.call-done = f32[96,256,64]{1,2,0:T(8,128)} async-done(((f32[3,256,64]{1,2,0:T(8,128)}), f32[96,256,64]{1,2,0:T(8,128)}) %all-gather.3.cloned.1.call-update) | async-done | bytes 6291472 | tf_op jit(solution)/shard_map/all_gather | solution.py:44
  167.3 3.2 reduce_sum.28
  170.9 2.1 collective-permute-start.10
  173.0 4.7 collective-permute-start.11
  178.0 0.9 pad_maximum_fusion.1
  178.9 1.9 collective-permute-done.11
  181.1 0.8 convolution_bitcast_fusion.9
  182.0 1.1 convolution_add_fusion.4
  183.1 1.1 convolution_add_fusion.3
  184.2 1.1 convolution_add_fusion.2
  185.3 79.8 %all-reduce.7.cloned.1.call-done = (f32[256,64]{0,1:T(8,128)}, f32[256,64]{0,1:T(8,128)}, f32[2,3,3,64,64]{3,4,1,2,0:T(8,128)}, f32[3,3,64,64]{3,2,1,0:T(8,128)}) async-done(((f32[256,64]{0,1:T(8,128)}, f32[256,64]{0,1:T(8,128)}, f32[2,3,3,64,64]{3,4,1,2,0:T(8,128)}, f32[3,3,64,64]{3,2,1,0:T(8,128)}), (f32[256,64]{0,1:T(8,128)}, f32[256,64]{0,1:T(8,128)}, f32[2,3,3,64,64]{3,4,1,2,0:T(8,128)}, ...) | async-done | bytes 573456 | tf_op jit(solution)/shard_map/psum | solution.py:276
  265.2 1.2 fusion.14
  266.4 1.1 copy.246
  267.5 17.1 %psum.76 = f32[64]{0:T(128)S(1)} all-reduce(f32[64]{0:T(128)S(1)} %copy-done.23), channel_id=1, replica_groups=mesh['row'=32,'col'=8] {'col'}, use_global_device_ids=true, to_apply=%region_9.10 | all-reduce | flops 64 | bytes 512 | tf_op jit(solution)/shard_map/psum | solution.py:276
  284.6 70.4 %psum.77 = f32[64]{0:T(128)} all-reduce(f32[64]{0:T(128)S(1)} %psum.76), channel_id=1, replica_groups=mesh['row'=32,'col'=8] {'row'}, use_global_device_ids=true, to_apply=%region_10.11 | all-reduce | flops 64 | bytes 512 | tf_op jit(solution)/shard_map/psum | solution.py:275
  355.0 0.7 fusion.178
  355.7 0.8 fusion.211
  356.5 199.4 %all-reduce.5.cloned.1.call-done = (f32[256,64]{0,1:T(8,128)}, f32[256,64]{0,1:T(8,128)}, f32[2,3,3,64,64]{3,4,1,2,0:T(8,128)}, f32[3,3,64,64]{3,2,1,0:T(8,128)}) async-done(((f32[256,64]{0,1:T(8,128)}, f32[256,64]{0,1:T(8,128)}, f32[2,3,3,64,64]{3,4,1,2,0:T(8,128)}, f32[3,3,64,64]{3,2,1,0:T(8,128)}), (f32[256,64]{0,1:T(8,128)}, f32[256,64]{0,1:T(8,128)}, f32[2,3,3,64,64]{3,4,1,2,0:T(8,128)}, ...) | async-done | bytes 573456 | tf_op jit(solution)/shard_map/psum | solution.py:275
  555.9 2.1 copy.247
  558.1 1.5 copy.333
  559.5 1.5 copy.334
  561.0 0.7 copy.335
  (134 shorter events, 16.5 us)
Async XLA Ops:
  7.2 17.1 %copy-start = (bf16[256,64]{0,1:T(8,128)(2,1)S(1)}, bf16[256,64]{0,1:T(8,128)(2,1)}, u32[]{:S(2)}) copy-start(bf16[256,64]{0,1:T(8,128)(2,1)} %param.12) | copy-start | bytes 98308
  7.2 16.1 %copy-start.1 = (bf16[64,16,256]{2,1,0:T(8,128)(2,1)S(1)}, bf16[64,16,256]{2,1,0:T(8,128)(2,1)}, u32[]{:S(2)}) copy-start(bf16[64,16,256]{2,1,0:T(8,128)(2,1)} %param.17) | copy-start | bytes 1572868
  7.2 11.7 %copy-start.17 = (s32[2]{0:T(128)S(1)}, s32[2]{0:T(128)}, u32[]{:S(2)}) copy-start(s32[2]{0:T(128)} %param.16) | copy-start | bytes 28
  7.2 16.0 %copy-start.3 = (bf16[2,3,3,64,64]{4,3,2,1,0:T(8,128)(2,1)S(1)}, bf16[2,3,3,64,64]{4,3,2,1,0:T(8,128)(2,1)}, u32[]{:S(2)}) copy-start(bf16[2,3,3,64,64]{4,3,2,1,0:T(8,128)(2,1)} %param.13) | copy-start | bytes 442372
  8.8 16.9 %all-to-all-start = ((bf16[8,2,64]{2,1,0:T(2,128)(2,1)}), bf16[8,2,64]{2,1,0:T(2,128)(2,1)S(1)}, u32[]{:S(2)}, u32[]{:S(2)}) async-start(bf16[8,2,64]{2,1,0:T(2,128)(2,1)} %broadcast_in_dim.12), calls=%async_computation | async-start | bytes 8192 | tf_op jit(solution)/shard_map/all_to_all | solution.py:11
  16.1 8.2 %copy-start.12 = (bf16[8,256]{1,0:T(8,128)(2,1)S(1)}, bf16[8,256]{1,0:T(8,128)(2,1)}, u32[]{:S(2)}) copy-start(bf16[8,256]{1,0:T(8,128)(2,1)} %param.10) | copy-start | bytes 12292
  16.2 45.8 %collective-permute-start.4 = (bf16[64,8,256]{2,0,1:T(8,128)(2,1)S(1)}, bf16[64,8,256]{2,0,1:T(8,128)(2,1)S(1)}, u32[]{:S(2)}, u32[]{:S(2)}) collective-permute-start(bf16[64,8,256]{2,0,1:T(8,128)(2,1)S(1)} %copy.319), channel_id=1, source_target_pairs={{0,8},{8,16},{16,24},{24,32},{32,40},{40,48},{48,56},{56,64},{64,7... | collective-permute-start | bytes 786440 | tf_op jit(solution)/shard_map/ppermute | solution.py:32
  17.6 44.7 %collective-permute-start.5 = (bf16[64,8,256]{2,0,1:T(8,128)(2,1)S(1)}, bf16[64,8,256]{2,0,1:T(8,128)(2,1)S(1)}, u32[]{:S(2)}, u32[]{:S(2)}) collective-permute-start(bf16[64,8,256]{2,0,1:T(8,128)(2,1)S(1)} %copy.320), channel_id=1, source_target_pairs={{8,0},{16,8},{24,16},{32,24},{40,32},{48,40},{56,48},{64,56},{72,6... | collective-permute-start | bytes 786440 | tf_op jit(solution)/shard_map/ppermute | solution.py:33
  25.7 25.0 %all-to-all-start.1 = ((bf16[32,2,256]{2,1,0:T(2,128)(2,1)}), bf16[32,2,256]{2,1,0:T(2,128)(2,1)S(1)}, u32[]{:S(2)}, u32[]{:S(2)}) async-start(bf16[32,2,256]{2,1,0:T(2,128)(2,1)} %reshape.293), calls=%async_computation.1 | async-start | bytes 65536 | tf_op jit(solution)/shard_map/all_to_all | solution.py:11
  40.9 126.5 %all-gather.3.cloned.1.call-start = ((), (), s32[]{:S(2)}) async-start(), calls=%async_computation.3 | async-start | bytes 6488064 | tf_op jit(solution)/shard_map/all_gather | solution.py:44
  40.9 8.2 %collective-permute-start = (bf16[16,64]{1,0:T(8,128)(2,1)S(1)}, bf16[16,64]{1,0:T(8,128)(2,1)S(1)}, u32[]{:S(2)}, u32[]{:S(2)}) collective-permute-start(bf16[16,64]{1,0:T(8,128)(2,1)S(1)} %bitcast.322), channel_id=1, source_target_pairs={{0,8},{8,16},{16,24},{24,32},{32,40},{40,48},{48,56},{56,64},{64,7... | collective-permute-start | bytes 6152 | tf_op jit(solution)/shard_map/ppermute | solution.py:32
  43.1 6.0 %collective-permute-start.1 = (bf16[16,64]{1,0:T(8,128)(2,1)S(1)}, bf16[16,64]{1,0:T(8,128)(2,1)S(1)}, u32[]{:S(2)}, u32[]{:S(2)}) collective-permute-start(bf16[16,64]{1,0:T(8,128)(2,1)S(1)} %bitcast.323), channel_id=1, source_target_pairs={{8,0},{16,8},{24,16},{32,24},{40,32},{48,40},{56,48},{64,56},{72,6... | collective-permute-start | bytes 6152 | tf_op jit(solution)/shard_map/ppermute | solution.py:33
  51.0 7.8 %collective-permute-start.2 = (bf16[16,64]{0,1:T(8,128)(2,1)S(1)}, bf16[16,64]{0,1:T(8,128)(2,1)S(1)}, u32[]{:S(2)}, u32[]{:S(2)}) collective-permute-start(bf16[16,64]{0,1:T(8,128)(2,1)S(1)} %copy.199), channel_id=1, source_target_pairs={{0,1},{1,2},{2,3},{3,4},{4,5},{5,6},{6,7},{8,9},{9,10},{10,11},{11... | collective-permute-start | bytes 6152 | tf_op jit(solution)/shard_map/ppermute | solution.py:32
  54.4 5.6 collective-permute-start.3
  62.2 7.3 %copy-start.18 = (pred[272,1]{0,1:T(4,128)(4,1)S(1)}, pred[272,1]{0,1:T(4,128)(4,1)}, u32[]{:S(2)}) copy-start(pred[272,1]{0,1:T(4,128)(4,1)} %get-tuple-element.93) | copy-start | bytes 820
  62.2 7.3 %copy-start.21 = (f32[64]{0:T(128)S(1)}, f32[64]{0:T(128)}, u32[]{:S(2)}) copy-start(f32[64]{0:T(128)} %param.14) | copy-start | bytes 772
  62.2 7.3 %copy-start.22 = (f32[3,32,64]{2,1,0:T(8,128)S(1)}, f32[3,32,64]{2,1,0:T(8,128)}, u32[]{:S(2)}) copy-start(f32[3,32,64]{2,1,0:T(8,128)} %convolution_bitcast_fusion.11) | copy-start | bytes 73732
  62.2 7.3 %copy-start.24 = (f32[32]{0:T(128)S(1)}, f32[32]{0:T(128)}, u32[]{:S(2)}) copy-start(f32[32]{0:T(128)} %and_convert_fusion) | copy-start | bytes 388
  62.6 17.7 %collective-permute-start.6 = (bf16[64,32,8]{2,0,1:T(8,128)(2,1)S(1)}, bf16[64,32,8]{2,0,1:T(8,128)(2,1)S(1)}, u32[]{:S(2)}, u32[]{:S(2)}) collective-permute-start(bf16[64,32,8]{2,0,1:T(8,128)(2,1)S(1)} %get-tuple-element.56), channel_id=1, source_target_pairs={{0,1},{1,2},{2,3},{3,4},{4,5},{5,6},{6,7},{8,9},{9,10},{10,11},{11... | collective-permute-start | bytes 98312 | tf_op jit(solution)/shard_map/ppermute | solution.py:32
  66.9 22.9 %collective-permute-start.7 = (bf16[64,32,8]{2,0,1:T(8,128)(2,1)S(1)}, bf16[64,32,8]{2,0,1:T(8,128)(2,1)S(1)}, u32[]{:S(2)}, u32[]{:S(2)}) collective-permute-start(bf16[64,32,8]{2,0,1:T(8,128)(2,1)S(1)} %get-tuple-element.57), channel_id=1, source_target_pairs={{1,0},{2,1},{3,2},{4,3},{5,4},{6,5},{7,6},{9,8},{10,9},{11,10},{12... | collective-permute-start | bytes 98312 | tf_op jit(solution)/shard_map/ppermute | solution.py:33
  74.2 16.7 %copy-start.4 = (bf16[3,3,64,64]{3,2,1,0:T(8,128)(2,1)S(1)}, bf16[3,3,64,64]{3,2,1,0:T(8,128)(2,1)}, u32[]{:S(2)}) copy-start(bf16[3,3,64,64]{3,2,1,0:T(8,128)(2,1)} %param.15) | copy-start | bytes 221188
  93.6 1.8 copy-start.20
  106.3 2.6 copy-start.5
  112.9 6.4 %copy-start.10 = (f32[1,64,64]{2,1,0:T(8,128)S(1)}, f32[1,64,64]{2,1,0:T(8,128)}, u32[]{:S(2)}) copy-start(f32[1,64,64]{2,1,0:T(8,128)} %convolution_bitcast_fusion.15) | copy-start | bytes 49156
  112.9 6.4 %copy-start.11 = (f32[1,64,64]{2,1,0:T(8,128)S(1)}, f32[1,64,64]{2,1,0:T(8,128)}, u32[]{:S(2)}) copy-start(f32[1,64,64]{2,1,0:T(8,128)} %convolution_bitcast_fusion.16) | copy-start | bytes 49156
  112.9 6.4 %copy-start.6 = (f32[1,3,64,64]{3,2,1,0:T(8,128)S(1)}, f32[1,3,64,64]{3,2,1,0:T(8,128)}, u32[]{:S(2)}) copy-start(f32[1,3,64,64]{3,2,1,0:T(8,128)} %maximum_bitcast_fusion.2) | copy-start | bytes 147460
  112.9 6.5 %copy-start.7 = (f32[1,3,64,64]{3,2,1,0:T(8,128)S(1)}, f32[1,3,64,64]{3,2,1,0:T(8,128)}, u32[]{:S(2)}) copy-start(f32[1,3,64,64]{3,2,1,0:T(8,128)} %maximum_bitcast_fusion.4) | copy-start | bytes 147460
  113.7 15.5 %copy-start.14 = (bf16[1,2,64]{2,1,0:T(2,128)(2,1)S(1)}, bf16[1,2,64]{2,1,0:T(2,128)(2,1)}, u32[]{:S(2)}) copy-start(bf16[1,2,64]{2,1,0:T(2,128)(2,1)} %get-tuple-element.80) | copy-start | bytes 772
  113.7 15.5 %copy-start.15 = (bf16[1,2,64]{2,1,0:T(2,128)(2,1)S(1)}, bf16[1,2,64]{2,1,0:T(2,128)(2,1)}, u32[]{:S(2)}) copy-start(bf16[1,2,64]{2,1,0:T(2,128)(2,1)} %get-tuple-element.81) | copy-start | bytes 772
  113.7 15.6 %copy-start.16 = (bf16[1,2,64]{2,1,0:T(2,128)(2,1)S(1)}, bf16[1,2,64]{2,1,0:T(2,128)(2,1)}, u32[]{:S(2)}) copy-start(bf16[1,2,64]{2,1,0:T(2,128)(2,1)} %get-tuple-element.82) | copy-start | bytes 772
  113.7 18.8 %copy-start.19 = (bf16[2,256]{1,0:T(2,128)(2,1)S(1)}, bf16[2,256]{1,0:T(2,128)(2,1)}, u32[]{:S(2)}) copy-start(bf16[2,256]{1,0:T(2,128)(2,1)} %param.9) | copy-start | bytes 3076
  114.5 9.9 %all-to-all-start.2 = ((f32[8,1,3072]{2,1,0:T(1,128)}), f32[8,1,3072]{2,1,0:T(1,128)S(1)}, u32[]{:S(2)}, u32[]{:S(2)}) async-start(f32[8,1,3072]{2,1,0:T(1,128)} %reshape.295), calls=%async_computation.2 | async-start | bytes 196608 | tf_op jit(solution)/shard_map/all_to_all | solution.py:11
  119.3 145.8 %all-reduce.7.cloned.1.call-start = ((), (), s32[]{:S(2)}) async-start(), calls=%async_computation.5 | async-start | bytes 2031616 | tf_op jit(solution)/shard_map/psum | solution.py:276
  126.3 3.3 collective-permute-start.8
  127.6 4.9 collective-permute-start.9
  170.9 10.2 %copy-start.13 = (bf16[8,256]{1,0:T(8,128)(2,1)S(1)}, bf16[8,256]{1,0:T(8,128)(2,1)}, u32[]{:S(2)}) copy-start(bf16[8,256]{1,0:T(8,128)(2,1)} %param.10) | copy-start | bytes 12292
  170.9 8.0 %collective-permute-start.10 = (f32[3,8,64]{1,2,0:T(8,128)S(1)}, f32[3,8,64]{1,2,0:T(8,128)S(1)}, u32[]{:S(2)}, u32[]{:S(2)}) collective-permute-start(f32[3,8,64]{1,2,0:T(8,128)S(1)} %get-tuple-element.65), channel_id=1, source_target_pairs={{0,1},{1,2},{2,3},{3,4},{4,5},{5,6},{6,7},{8,9},{9,10},{10,11},{11... | collective-permute-start | bytes 18440 | tf_op jit(solution)/shard_map/ppermute | solution.py:32
  173.0 7.8 %collective-permute-start.11 = (f32[3,8,64]{1,2,0:T(8,128)S(1)}, f32[3,8,64]{1,2,0:T(8,128)S(1)}, u32[]{:S(2)}, u32[]{:S(2)}) collective-permute-start(f32[3,8,64]{1,2,0:T(8,128)S(1)} %get-tuple-element.66), channel_id=1, source_target_pairs={{1,0},{2,1},{3,2},{4,3},{5,4},{6,5},{7,6},{9,8},{10,9},{11,10},{12... | collective-permute-start | bytes 18440 | tf_op jit(solution)/shard_map/ppermute | solution.py:33
  178.0 3.9 copy-start.2
  181.9 374.0 %all-reduce.5.cloned.1.call-start = ((), (), s32[]{:S(2)}) async-start(), calls=%async_computation.4 | async-start | bytes 2031616 | tf_op jit(solution)/shard_map/psum | solution.py:275
  265.2 2.3 copy-start.23
  265.2 89.8 %copy-start.9 = (bf16[256,64]{0,1:T(8,128)(2,1)S(1)}, bf16[256,64]{0,1:T(8,128)(2,1)}, u32[]{:S(2)}) copy-start(bf16[256,64]{0,1:T(8,128)(2,1)} %param.11) | copy-start | bytes 98308
  555.9 5.1 copy-start.8
Sparse Core Ops, SparseCore 0:
  97.4 69.8 all-gather.2
  182.0 83.0 all-reduce.6
  268.0 287.8 all-reduce.4
